TPU v7x, 32 devices: a whole 2x2x4 slice. The times are simulated.
32 devices in a mesh: groups: 1, gx: 8 (over z, y), gy: 2 (over core), segment: 2 (over x).
Axes of the slice: x: 2, y: 2, z: 4, core: 2. Of those that a mesh axis runs over, the one named last changes fastest.
Arguments:
- activations: bfloat16 [2, 8, 128, 128, 128], P('segment', 'groups', 'gx', 'gy'), may hold values from -6 to 6
- cotangent: bfloat16 [8, 128, 128, 128], P('groups', 'gx', 'gy'), may hold values from -6 to 6
- spectral_weights: float32 [2, 32, 32, 8, 8, 32], P('segment', 'gy', 'gx'), may hold values from -6 to 6
- pointwise: float32 [2, 8, 8], P('segment'), may hold values from -2 to 2
- channel_bias: float32 [2, 8], P('segment'), may hold values from -3 to 3
Outputs:
- input_grads: bfloat16 [2, 8, 128, 128, 128], P('segment', 'groups', 'gx', 'gy')
- spectral_grads: float32 [2, 32, 32, 8, 8, 32], P('segment', 'gy', 'gx', 'groups')
All inputs are finite; a program needn't handle non-finite values.
Results may differ from a plain program's by a relative error of at most 0.0042.
Values may be sent and summed in bfloat16 or wider, within the bound.
A program may use at most 64 MiB of HBM per device.

v0:
```python
import math
import jax
import jax.numpy as jnp
from jax import lax
from jax.sharding import PartitionSpec as P

MODES = 32
highest = lax.Precision.HIGHEST


def from_behind(block, axis, distance):
    devices = range(lax.axis_size(axis))
    route = [(i - distance, i) for i in devices if i - distance in devices]
    return lax.ppermute(block, axis, route)


def trig_basis(length, mode_count):
    half = mode_count // 2
    freqs = jnp.arange(half, dtype=jnp.int32)[:, None]
    points = jnp.arange(length, dtype=jnp.int32)[None, :]
    step_angle = 2.0 * math.pi / length
    cosine = jnp.cos((freqs * points % length).astype(jnp.float32) * step_angle)
    sine = jnp.sin(((freqs + 1) * points % length).astype(jnp.float32) * step_angle)
    rows_all = jnp.concatenate([cosine, sine], axis=0)
    scales = jnp.where(
        jnp.arange(mode_count) == 0, 1.0 / math.sqrt(length), math.sqrt(2.0 / length)
    ).astype(jnp.float32)
    return rows_all * scales[:, None]


def gelu_slope(value):
    normal_cdf = 0.5 * (1.0 + jax.scipy.special.erf(value * 0.7071067811865476))
    return normal_cdf + value * jnp.exp(-0.5 * value * value) * 0.3989422804014327


def channel_mix(matrix, field):
    return jnp.sum(matrix[:, :, None, None, None] * field[None], axis=1)


def body(activations, cotangent, spectral_weights, pointwise, channel_bias):
    inputs = activations[0].astype(jnp.float32)
    channels, rows_x, rows_y, length_z = inputs.shape
    count_x = lax.axis_size("gx")
    count_y = lax.axis_size("gy")
    mode_count = MODES
    along_x = trig_basis(rows_x * count_x, mode_count)
    along_z = trig_basis(length_z, mode_count)
    along_y = lax.dynamic_slice_in_dim(
        trig_basis(rows_y * count_y, mode_count), lax.axis_index("gy") * rows_y, rows_y, 1
    )
    weights = spectral_weights[0]
    mixing = pointwise[0]
    mixing_back = jnp.transpose(mixing)

    def analyse(field):
        third = jnp.einsum("ixyz,cz->cixy", field, along_z, precision=highest)
        partial_value = jnp.einsum(
            "cixy,ax->ciay",
            lax.all_to_all(third, "gx", split_axis=0, concat_axis=2, tiled=True),
            along_x,
            precision=highest,
        )
        return lax.psum_scatter(
            jnp.einsum("ciay,jy->jcia", partial_value, along_y, precision=highest),
            "gy",
            scatter_dimension=0,
            tiled=True,
        )

    def synthesise(spectrum):
        second = jnp.einsum(
            "jcia,jy->ciay",
            lax.all_gather(spectrum, "gy", axis=0, tiled=True),
            along_y,
            precision=highest,
        )
        spread = jnp.einsum("ciay,ax->cixy", second, along_x, precision=highest)
        return jnp.einsum(
            "cixy,cz->ixyz",
            lax.all_to_all(spread, "gx", split_axis=2, concat_axis=0, tiled=True),
            along_z,
            precision=highest,
        )

    input_modes = analyse(inputs)
    mixed = jnp.einsum("jcioa,jcia->jcoa", weights, input_modes, precision=highest)
    pre_act = channel_mix(mixing, inputs)
    pre_act = pre_act + channel_bias[0][:, None, None, None] + synthesise(mixed)
    slope_field = gelu_slope(pre_act)
    segment_index = lax.axis_index("segment")
    segment_count = lax.axis_size("segment")
    incoming = cotangent
    kept_grad = jnp.zeros(cotangent.shape, jnp.bfloat16)
    kept_modes = jnp.zeros(input_modes.shape, jnp.float32)
    for turn_index in range(segment_count):
        active = segment_index == segment_count - 1 - turn_index
        signal = incoming.astype(jnp.float32) * slope_field
        grad_modes = analyse(signal)
        back = jnp.einsum("jcioa,jcoa->jcia", weights, grad_modes, precision=highest)
        input_grad = channel_mix(mixing_back, signal) + synthesise(back)
        input_grad = input_grad.astype(jnp.bfloat16)
        kept_grad = jnp.where(active, input_grad, kept_grad)
        kept_modes = jnp.where(active, grad_modes, kept_modes)
        if turn_index + 1 < segment_count:
            incoming = from_behind(input_grad, "segment", -1)
    weight_grad = jnp.einsum("jcia,jcoa->jcioa", input_modes, kept_modes, precision=highest)
    return (kept_grad[None], weight_grad[None])


def solution(mesh):
    return jax.shard_map(
        body,
        mesh=mesh,
        in_specs=(
            P("segment", "groups", "gx", "gy", None),
            P("groups", "gx", "gy", None),
            P("segment", "gy", "gx", None, None, None),
            P("segment", None, None),
            P("segment", None),
        ),
        out_specs=(
            P("segment", "groups", "gx", "gy", None),
            P("segment", "gy", "gx", "groups", None, None),
        ),
        check_vma=False,
    )
```

profile of v0, /device:TPU:0, one launch (start us, length us, event | category | flops | bytes accessed | tf_op | source)
XLA Modules:
  0.0 441.0 jit_solution(13617722540841769567)
XLA Ops:
  7.4 7.4 %fusion.7 = f32[32,8,16,64]{3,0,2,1:T(8,128)S(1)} fusion(bf16[1,8,16,64,128]{4,3,2,1,0:T(8,128)(2,1)} %param.5, f32[32,128]{1,0:T(8,128)S(1)} %maximum_multiply_fusion), kind=kOutput, calls=%fused_computation.18 | convolution fusion | flops 402653184 | bytes 3162112 | tf_op jit(solution)/shard_map/ixyz,cz->cixy/dot_general | solution.py:56
  18.1 7.3 %all-to-all-start = ((f32[8,1,32768]{2,1,0:T(1,128)}), f32[8,1,32768]{2,1,0:T(1,128)S(1)}, u32[]{:S(2)}, u32[]{:S(2)}) async-start(f32[8,1,32768]{2,1,0:T(1,128)} %reshape.27), calls=%async_computation | async-start | bytes 2097152 | tf_op jit(solution)/shard_map/all_to_all | solution.py:59
  25.4 25.7 %all-to-all-done = f32[8,1,32768]{2,1,0:T(1,128)S(1)} async-done(((f32[8,1,32768]{2,1,0:T(1,128)}), f32[8,1,32768]{2,1,0:T(1,128)S(1)}, u32[]{:S(2)}, u32[]{:S(2)}) %all-to-all-start) | async-done | bytes 1048608 | tf_op jit(solution)/shard_map/all_to_all | solution.py:59
  60.4 7.1 %reduce-scatter.4.cloned.1.call-done = f32[16,4,8,32]{3,0,2,1:T(8,128)} async-done(((f32[32,4,8,32]{3,0,2,1:T(8,128)}), f32[16,4,8,32]{3,0,2,1:T(8,128)}) %reduce-scatter.4.cloned.1.call-update) | async-done | bytes 65552 | tf_op jit(solution)/shard_map/reduce_scatter | solution.py:63
  80.6 5.7 %all-to-all-start.1 = ((f32[8,1,32768]{2,1,0:T(1,128)}), f32[8,1,32768]{2,1,0:T(1,128)}, u32[]{:S(2)}, u32[]{:S(2)}) async-start(f32[8,1,32768]{2,1,0:T(1,128)} %reshape.29), calls=%async_computation.2 | async-start | bytes 2097152 | tf_op jit(solution)/shard_map/all_to_all | solution.py:80
  90.5 7.2 %multiply_reduce_fusion.2 = f32[8,16,64,128]{3,2,1,0:T(8,128)} fusion(f32[8,16,64,128]{3,2,1,0:T(8,128)} %bitcast_convert_fusion, f32[8,8]{1,0:T(8,128)S(1)} %bitcast.160), kind=kLoop, calls=%fused_computation.2 | loop fusion | flops 15728640 | bytes 8388864 | tf_op jit(solution)/shard_map/reduce_sum | solution.py:37
  97.6 15.1 %all-to-all-done.1 = f32[8,1,32768]{2,1,0:T(1,128)} async-done(((f32[8,1,32768]{2,1,0:T(1,128)}), f32[8,1,32768]{2,1,0:T(1,128)}, u32[]{:S(2)}, u32[]{:S(2)}) %all-to-all-start.1) | async-done | bytes 1048608 | tf_op jit(solution)/shard_map/all_to_all | solution.py:80
  112.8 4.3 reduce.7
  122.1 11.8 %convert_multiply_fusion.1 = (f32[8,16,64,128]{3,2,1,0:T(8,128)S(1)}, f32[8,16,64,128]{3,2,1,0:T(8,128)}) fusion(bf16[8,16,64,128]{3,2,1,0:T(8,128)(2,1)} %param.6, f32[32,8,16,64]{3,0,2,1:T(8,128)S(1)} %bitcast.153, f32[32,128]{1,0:T(8,128)S(1)} %maximum_multiply_fusion, f32[8,16,64,128]{3,2,1,0:T(8,128)S(1)} %copy-done.6, f32[8]{0:T(128)S(1)} %bitcast.162), kind=kOutput, calls=%fused_computation.11 | convolution fusion | flops 415236096 | bytes 15745056 | tf_op jit(solution)/shard_map/cixy,cz->ixyz/dot_general | solution.py:78
  133.9 11.3 %fusion.32 = f32[32,8,16,64]{3,0,2,1:T(8,128)S(1)} fusion(f32[8,16,64,128]{3,2,1,0:T(8,128)S(1)} %get-tuple-element.2, f32[32,128]{1,0:T(8,128)S(1)} %maximum_multiply_fusion), kind=kOutput, calls=%fused_computation.54 | convolution fusion | flops 402653184 | bytes 5259264 | tf_op jit(solution)/shard_map/ixyz,cz->cixy/dot_general | solution.py:56
  150.3 29.7 %all_to_all.108 = f32[8,1,32768]{2,1,0:T(1,128)} all-to-all(f32[8,1,32768]{2,1,0:T(1,128)S(1)} %reshape.31), channel_id=1, replica_groups=mesh['groups'=1,'gx'=8,'gy'=2,'segment'=2] {'gx'}, dimensions={0} | all-to-all | bytes 2097152 | tf_op jit(solution)/shard_map/all_to_all | solution.py:59
  192.8 7.1 %reduce-scatter.6.cloned.1.call-done = f32[16,4,8,32]{3,0,2,1:T(8,128)} async-done(((f32[32,4,8,32]{3,0,2,1:T(8,128)}), f32[16,4,8,32]{3,0,2,1:T(8,128)}) %reduce-scatter.6.cloned.1.call-update) | async-done | bytes 65552 | tf_op jit(solution)/shard_map/reduce_scatter | solution.py:63
  213.2 5.7 %all-to-all-start.3 = ((f32[8,1,32768]{2,1,0:T(1,128)}), f32[8,1,32768]{2,1,0:T(1,128)}, u32[]{:S(2)}, u32[]{:S(2)}) async-start(f32[8,1,32768]{2,1,0:T(1,128)} %reshape.33), calls=%async_computation.5 | async-start | bytes 2097152 | tf_op jit(solution)/shard_map/all_to_all | solution.py:80
  219.4 7.2 %multiply_reduce_fusion.1 = f32[8,16,64,128]{3,2,1,0:T(8,128)} fusion(f32[8,16,64,128]{3,2,1,0:T(8,128)} %copy-done.1, f32[8,8]{1,0:T(8,128)S(1)} %copy.49), kind=kLoop, calls=%fused_computation.1 | loop fusion | flops 15728640 | bytes 8388864 | tf_op jit(solution)/shard_map/reduce_sum | solution.py:37
  226.6 18.6 %all-to-all-done.3 = f32[8,1,32768]{2,1,0:T(1,128)} async-done(((f32[8,1,32768]{2,1,0:T(1,128)}), f32[8,1,32768]{2,1,0:T(1,128)}, u32[]{:S(2)}, u32[]{:S(2)}) %all-to-all-start.3) | async-done | bytes 1048608 | tf_op jit(solution)/shard_map/all_to_all | solution.py:80
  254.6 7.1 %add_convert_fusion.1 = bf16[8,16,64,128]{3,2,1,0:T(8,128)(2,1)S(1)} fusion(f32[8,16,64,128]{3,2,1,0:T(8,128)S(1)} %copy-done.4, f32[32,8,16,64]{3,0,2,1:T(8,128)S(1)} %bitcast.152, f32[32,128]{1,0:T(8,128)S(1)} %maximum_multiply_fusion), kind=kOutput, calls=%fused_computation.10 | convolution fusion | flops 404750336 | bytes 7356416 | tf_op jit(solution)/shard_map/cixy,cz->ixyz/dot_general | solution.py:78
  263.1 47.1 %collective-permute-done = bf16[8,16,64,128]{3,2,1,0:T(8,128)(2,1)S(1)} collective-permute-done((bf16[8,16,64,128]{3,2,1,0:T(8,128)(2,1)S(1)}, bf16[8,16,64,128]{3,2,1,0:T(8,128)(2,1)S(1)}, u32[]{:S(2)}, u32[]{:S(2)}) %collective-permute-start) | collective-permute-done | bytes 2097184 | tf_op jit(solution)/shard_map/ppermute | solution.py:14
  311.3 11.3 %fusion.27 = f32[32,8,16,64]{3,0,2,1:T(8,128)S(1)} fusion(f32[8,16,64,128]{3,2,1,0:T(8,128)S(1)} %convert_multiply_fusion, f32[32,128]{1,0:T(8,128)S(1)} %maximum_multiply_fusion), kind=kOutput, calls=%fused_computation.49 | convolution fusion | flops 402653184 | bytes 5259264 | tf_op jit(solution)/shard_map/ixyz,cz->cixy/dot_general | solution.py:56
  327.8 29.7 %all_to_all.109 = f32[8,1,32768]{2,1,0:T(1,128)} all-to-all(f32[8,1,32768]{2,1,0:T(1,128)S(1)} %reshape.35), channel_id=1, replica_groups=mesh['groups'=1,'gx'=8,'gy'=2,'segment'=2] {'gx'}, dimensions={0} | all-to-all | bytes 2097152 | tf_op jit(solution)/shard_map/all_to_all | solution.py:59
  370.4 6.1 %reduce-scatter.8.cloned.1.call-done = f32[16,4,8,32]{3,0,2,1:T(8,128)} async-done(((f32[32,4,8,32]{3,0,2,1:T(8,128)}), f32[16,4,8,32]{3,0,2,1:T(8,128)}) %reduce-scatter.8.cloned.1.call-update) | async-done | bytes 65552 | tf_op jit(solution)/shard_map/reduce_scatter | solution.py:63
  387.6 6.0 %all-to-all-start.5 = ((f32[8,1,32768]{2,1,0:T(1,128)}), f32[8,1,32768]{2,1,0:T(1,128)S(1)}, u32[]{:S(2)}, u32[]{:S(2)}) async-start(f32[8,1,32768]{2,1,0:T(1,128)} %reshape.37), calls=%async_computation.8 | async-start | bytes 2097152 | tf_op jit(solution)/shard_map/all_to_all | solution.py:80
  393.7 7.2 %multiply_reduce_fusion = f32[8,16,64,128]{3,2,1,0:T(8,128)} fusion(f32[8,16,64,128]{3,2,1,0:T(8,128)} %copy-done, f32[8,8]{1,0:T(8,128)S(1)} %copy.49), kind=kLoop, calls=%fused_computation | loop fusion | flops 15728640 | bytes 8388864 | tf_op jit(solution)/shard_map/reduce_sum | solution.py:37
  402.7 17.2 %all-to-all-done.5 = f32[8,1,32768]{2,1,0:T(1,128)S(1)} async-done(((f32[8,1,32768]{2,1,0:T(1,128)}), f32[8,1,32768]{2,1,0:T(1,128)S(1)}, u32[]{:S(2)}, u32[]{:S(2)}) %all-to-all-start.5) | async-done | bytes 1048608 | tf_op jit(solution)/shard_map/all_to_all | solution.py:80
  426.0 8.0 %select_bitcast_fusion = bf16[1,8,16,64,128]{4,3,2,1,0:T(8,128)(2,1)} fusion(bf16[8,16,64,128]{3,2,1,0:T(8,128)(2,1)} %copy-done.7, pred[]{:T(512)S(6)} %eq.24, pred[]{:T(512)S(6)} %eq.22, f32[8,16,64,128]{3,2,1,0:T(8,128)S(1)} %copy-done.3, f32[32,8,16,64]{3,0,2,1:T(8,128)S(1)} %bitcast.151, f32[32,128]{1,0:T(8,128)S(1)} %maximum_multiply_fusion), kind=kOutput, calls=%fused_computation.22 | convolution fusion | flops 406847488 | bytes 9453570 | tf_op jit(solution)/shard_map/cixy,cz->ixyz/dot_general | solution.py:78
  (92 shorter events, 115.1 us)
Async XLA Ops:
  18.1 33.0 %all-to-all-start = ((f32[8,1,32768]{2,1,0:T(1,128)}), f32[8,1,32768]{2,1,0:T(1,128)S(1)}, u32[]{:S(2)}, u32[]{:S(2)}) async-start(f32[8,1,32768]{2,1,0:T(1,128)} %reshape.27), calls=%async_computation | async-start | bytes 2097152 | tf_op jit(solution)/shard_map/all_to_all | solution.py:59
  25.4 42.1 %reduce-scatter.4.cloned.1.call-start = ((), (), s32[]{:S(2)}) async-start(), calls=%async_computation.9 | async-start | bytes 786432 | tf_op jit(solution)/shard_map/reduce_scatter | solution.py:63
  55.9 12.7 %copy-start.2 = (f32[1,16,4,8,8,32]{5,4,3,2,1,0:T(8,128)S(1)}, f32[1,16,4,8,8,32]{5,4,3,2,1,0:T(8,128)}, u32[]{:S(2)}) copy-start(f32[1,16,4,8,8,32]{5,4,3,2,1,0:T(8,128)} %param.7) | copy-start | bytes 1572868
  80.6 32.1 %all-to-all-start.1 = ((f32[8,1,32768]{2,1,0:T(1,128)}), f32[8,1,32768]{2,1,0:T(1,128)}, u32[]{:S(2)}, u32[]{:S(2)}) async-start(f32[8,1,32768]{2,1,0:T(1,128)} %reshape.29), calls=%async_computation.2 | async-start | bytes 2097152 | tf_op jit(solution)/shard_map/all_to_all | solution.py:80
  86.4 4.1 copy-start.10
  86.4 113.6 %reduce-scatter.6.cloned.1.call-start = ((), (), s32[]{:S(2)}) async-start(), calls=%async_computation.10 | async-start | bytes 786432 | tf_op jit(solution)/shard_map/reduce_scatter | solution.py:63
  119.2 2.8 copy-start.6
  119.2 2.8 copy-start.11
  133.9 11.4 %copy-start.1 = (f32[8,16,64,128]{3,2,1,0:T(8,128)}, f32[8,16,64,128]{3,2,1,0:T(8,128)S(1)}, u32[]{:S(2)}) copy-start(f32[8,16,64,128]{3,2,1,0:T(8,128)S(1)} %get-tuple-element.2) | copy-start | bytes 12582916
  213.2 32.1 %all-to-all-start.3 = ((f32[8,1,32768]{2,1,0:T(1,128)}), f32[8,1,32768]{2,1,0:T(1,128)}, u32[]{:S(2)}, u32[]{:S(2)}) async-start(f32[8,1,32768]{2,1,0:T(1,128)} %reshape.33), calls=%async_computation.5 | async-start | bytes 2097152 | tf_op jit(solution)/shard_map/all_to_all | solution.py:80
  218.9 157.6 %reduce-scatter.8.cloned.1.call-start = ((), (), s32[]{:S(2)}) async-start(), calls=%async_computation.11 | async-start | bytes 786432 | tf_op jit(solution)/shard_map/reduce_scatter | solution.py:63
  251.7 2.8 copy-start.4
  254.6 55.7 %copy-start.5 = (f32[8,16,64,128]{3,2,1,0:T(8,128)S(1)}, f32[8,16,64,128]{3,2,1,0:T(8,128)}, u32[]{:S(2)}) copy-start(f32[8,16,64,128]{3,2,1,0:T(8,128)} %get-tuple-element.3) | copy-start | bytes 12582916
  261.6 48.6 %copy-start.7 = (bf16[8,16,64,128]{3,2,1,0:T(8,128)(2,1)}, bf16[8,16,64,128]{3,2,1,0:T(8,128)(2,1)S(1)}, u32[]{:S(2)}) copy-start(bf16[8,16,64,128]{3,2,1,0:T(8,128)(2,1)S(1)} %add_convert_fusion.1) | copy-start | bytes 6291460
  261.6 48.6 %collective-permute-start = (bf16[8,16,64,128]{3,2,1,0:T(8,128)(2,1)S(1)}, bf16[8,16,64,128]{3,2,1,0:T(8,128)(2,1)S(1)}, u32[]{:S(2)}, u32[]{:S(2)}) collective-permute-start(bf16[8,16,64,128]{3,2,1,0:T(8,128)(2,1)S(1)} %add_convert_fusion.1), channel_id=1, source_target_pairs={{1,0},{3,2},{5,4},{7,6},{9,8},{11,10},{13,12},{15,14},{17,16},{19,... | collective-permute-start | bytes 6291464 | tf_op jit(solution)/shard_map/ppermute | solution.py:14
  311.3 11.4 %copy-start = (f32[8,16,64,128]{3,2,1,0:T(8,128)}, f32[8,16,64,128]{3,2,1,0:T(8,128)S(1)}, u32[]{:S(2)}) copy-start(f32[8,16,64,128]{3,2,1,0:T(8,128)S(1)} %convert_multiply_fusion) | copy-start | bytes 12582916
  387.6 32.3 %all-to-all-start.5 = ((f32[8,1,32768]{2,1,0:T(1,128)}), f32[8,1,32768]{2,1,0:T(1,128)S(1)}, u32[]{:S(2)}, u32[]{:S(2)}) async-start(f32[8,1,32768]{2,1,0:T(1,128)} %reshape.37), calls=%async_computation.8 | async-start | bytes 2097152 | tf_op jit(solution)/shard_map/all_to_all | solution.py:80
  393.7 7.2 %copy-start.8 = (f32[16,4,8,32]{3,0,2,1:T(8,128)S(1)}, f32[16,4,8,32]{3,0,2,1:T(8,128)}, u32[]{:S(2)}) copy-start(f32[16,4,8,32]{3,0,2,1:T(8,128)} %reduce-scatter.6.cloned.1.call-done) | copy-start | bytes 196612
  393.7 7.2 %copy-start.9 = (f32[16,4,8,32]{3,0,2,1:T(8,128)S(1)}, f32[16,4,8,32]{3,0,2,1:T(8,128)}, u32[]{:S(2)}) copy-start(f32[16,4,8,32]{3,0,2,1:T(8,128)} %reduce-scatter.8.cloned.1.call-done) | copy-start | bytes 196612
  423.8 2.2 copy-start.3
Sparse Core Ops, SparseCore 0:
  60.5 6.9 reduce-scatter.3
  193.0 6.9 reduce-scatter.5
  370.5 5.9 reduce-scatter.7
where the time goes:
time: 450 us; the launch traced here: 441 us
  waiting for transfers between devices  144 us (32%)
  matrix products  79.5 us (18%)
  blocking collectives  66.3 us (15%)
  local copies, waits for them, and re-layouts  55.7 us (12%)
  other arithmetic  53.9 us (12%)
  starting transfers between devices  26.8 us (6%)
  between operations  14.6 us (3%)
    all_to_all x2, blocking collectives, analyse(): lax.all_to_all(third, 'gx', split_axis=0, concat_axis=2, tiled=True)  59.4 us
    all_to_all x3, waiting for transfers between devices, synthesise(): lax.all_to_all(spread, 'gx', split_axis=2, concat_axis=0, tiled=True)  51 us
    ppermute x1, waiting for transfers between devices, from_behind(): return lax.ppermute(block, axis, route)  47.1 us
    unnamed x39, local copies, waits for them, and re-layouts  32.2 us
    dot_general x3, matrix products, analyse(): third = jnp.einsum('ixyz,cz->cixy', field, along_z, precision=highest)  30.1 us
    dot_general x3, matrix products, synthesise(): jnp.einsum('cixy,cz->ixyz', lax.all_to_all(spread, 'gx', split_axis=2, co...  26.9 us
    all_to_all x1, waiting for transfers between devices, analyse(): lax.all_to_all(third, 'gx', split_axis=0, concat_axis=2, tiled=True)  25.7 us
    reduce_sum x3, other arithmetic, channel_mix(): return jnp.sum(matrix[:, :, None, None, None] * field[None], axis=1)  21.6 us
  transfers between devices with their start and end apart: 8, of which 8 were waited for; matrix products, arithmetic and copies ran while one was open for 6% of the time, Pallas kernels for 0%

commit v1 on v0

--- a/solution.py
+++ b/solution.py
@@ -77,7 +77,12 @@
         spread = jnp.einsum("ciay,ax->cixy", second, along_x, precision=highest)
         return jnp.einsum(
             "cixy,cz->ixyz",
-            lax.all_to_all(spread, "gx", split_axis=2, concat_axis=0, tiled=True),
+            jnp.concatenate(
+                lax.all_to_all(
+                    jnp.stack(jnp.split(spread, lax.axis_size("gx"), axis=2)), "gx", 0, 0
+                ),
+                axis=0,
+            ),
             along_z,
             precision=highest,
         )

time: 450 us -> 531 us (1.18)
  local copies, waits for them, and re-layouts: 55.7 us -> 135 us
    another operation x0 -> x30, local copies, waits for them, and re-layouts: none -> 64.2 us  [synthesise(): jnp.stack(jnp.split(spread, lax.axis_size('gx'), axis=2))]
    unnamed x39 -> x86, local copies, waits for them, and re-layouts: 32.2 us -> 52.3 us
    transpose x3 -> x0, local copies, waits for them, and re-layouts: 7.47 us -> none  [synthesise(): spread = jnp.einsum('ciay,ax->cixy', second, along_x, precision=highest)]
  transfers between devices with their start and end apart: 8 -> 8, of which waited for: 8 -> 8; matrix products, arithmetic and copies ran while one was open for 6% -> 5% of each run, Pallas kernels for 0% -> 0%
where the time goes in v1:
time: 531 us; the launch traced here: 521 us
  waiting for transfers between devices  144 us (27%)
  local copies, waits for them, and re-layouts  135 us (25%)
  matrix products  79.6 us (15%)
  blocking collectives  66.9 us (13%)
  other arithmetic  54.3 us (10%)
  starting transfers between devices  26.7 us (5%)
  between operations  14.4 us (3%)
    another operation x30, local copies, waits for them, and re-layouts, synthesise(): jnp.stack(jnp.split(spread, lax.axis_size('gx'), axis=2))  64.2 us
    all_to_all x2, blocking collectives, analyse(): lax.all_to_all(third, 'gx', split_axis=0, concat_axis=2, tiled=True)  59.8 us
    unnamed x86, local copies, waits for them, and re-layouts  52.3 us
    all_to_all x3, waiting for transfers between devices, synthesise(): lax.all_to_all(jnp.stack(jnp.split(spread, lax.axis_size('gx'), axis=2)),...  51 us
    ppermute x1, waiting for transfers between devices, from_behind(): return lax.ppermute(block, axis, route)  47.1 us
    dot_general x3, matrix products, analyse(): third = jnp.einsum('ixyz,cz->cixy', field, along_z, precision=highest)  30.1 us
    dot_general x3, matrix products, synthesise(): jnp.einsum('cixy,cz->ixyz', jnp.concatenate(lax.all_to_all(jnp.stack(jnp....  27 us
    all_to_all x1, waiting for transfers between devices, analyse(): lax.all_to_all(third, 'gx', split_axis=0, concat_axis=2, tiled=True)  25.7 us
  transfers between devices with their start and end apart: 8, of which 8 were waited for; matrix products, arithmetic and copies ran while one was open for 5% of the time, Pallas kernels for 0%

profile of v1, /device:TPU:0, one launch (start us, length us, event | category | flops | bytes accessed | tf_op | source)
XLA Modules:
  0.0 521.2 jit_solution(13975355532718205358)
XLA Ops:
  7.4 7.4 %fusion.7 = f32[32,8,16,64]{3,0,2,1:T(8,128)S(1)} fusion(bf16[1,8,16,64,128]{4,3,2,1,0:T(8,128)(2,1)} %param.5, f32[32,128]{1,0:T(8,128)S(1)} %maximum_multiply_fusion), kind=kOutput, calls=%fused_computation.18 | convolution fusion | flops 402653184 | bytes 3162112 | tf_op jit(solution)/shard_map/ixyz,cz->cixy/dot_general | solution.py:56
  18.1 7.3 %all-to-all-start = ((f32[8,1,32768]{2,1,0:T(1,128)}), f32[8,1,32768]{2,1,0:T(1,128)S(1)}, u32[]{:S(2)}, u32[]{:S(2)}) async-start(f32[8,1,32768]{2,1,0:T(1,128)} %reshape.39), calls=%async_computation | async-start | bytes 2097152 | tf_op jit(solution)/shard_map/all_to_all | solution.py:59
  25.4 25.7 %all-to-all-done = f32[8,1,32768]{2,1,0:T(1,128)S(1)} async-done(((f32[8,1,32768]{2,1,0:T(1,128)}), f32[8,1,32768]{2,1,0:T(1,128)S(1)}, u32[]{:S(2)}, u32[]{:S(2)}) %all-to-all-start) | async-done | bytes 1048608 | tf_op jit(solution)/shard_map/all_to_all | solution.py:59
  60.5 7.1 %reduce-scatter.4.cloned.1.call-done = f32[16,4,8,32]{3,0,2,1:T(8,128)} async-done(((f32[32,4,8,32]{3,0,2,1:T(8,128)}), f32[16,4,8,32]{3,0,2,1:T(8,128)}) %reduce-scatter.4.cloned.1.call-update) | async-done | bytes 65552 | tf_op jit(solution)/shard_map/reduce_scatter | solution.py:63
  109.6 5.7 %all-to-all-start.1 = ((f32[8,1,32768]{2,1,0:T(1,128)}), f32[8,1,32768]{2,1,0:T(1,128)}, u32[]{:S(2)}, u32[]{:S(2)}) async-start(f32[8,1,32768]{2,1,0:T(1,128)} %reshape.41), calls=%async_computation.2 | async-start | bytes 2097152 | tf_op jit(solution)/shard_map/all_to_all | solution.py:81
  119.6 7.2 %multiply_reduce_fusion.2 = f32[8,16,64,128]{3,2,1,0:T(8,128)} fusion(f32[8,16,64,128]{3,2,1,0:T(8,128)} %bitcast_convert_fusion, f32[8,8]{1,0:T(8,128)S(1)} %bitcast.187), kind=kLoop, calls=%fused_computation.2 | loop fusion | flops 15728640 | bytes 8388864 | tf_op jit(solution)/shard_map/reduce_sum | solution.py:37
  126.7 14.9 %all-to-all-done.1 = f32[8,1,32768]{2,1,0:T(1,128)} async-done(((f32[8,1,32768]{2,1,0:T(1,128)}), f32[8,1,32768]{2,1,0:T(1,128)}, u32[]{:S(2)}, u32[]{:S(2)}) %all-to-all-start.1) | async-done | bytes 1048608 | tf_op jit(solution)/shard_map/all_to_all | solution.py:81
  151.3 11.9 %convert_multiply_fusion.1 = (f32[8,16,64,128]{3,2,1,0:T(8,128)S(1)}, f32[8,16,64,128]{3,2,1,0:T(8,128)}) fusion(bf16[8,16,64,128]{3,2,1,0:T(8,128)(2,1)} %param.6, f32[32,8,16,64]{3,0,2,1:T(8,128)S(1)} %bitcast.180, f32[32,128]{1,0:T(8,128)S(1)} %maximum_multiply_fusion, f32[8,16,64,128]{3,2,1,0:T(8,128)S(1)} %copy-done.6, f32[8]{0:T(128)S(1)} %bitcast.189), kind=kOutput, calls=%fused_computation.11 | convolution fusion | flops 415236096 | bytes 15745056 | tf_op jit(solution)/shard_map/cixy,cz->ixyz/dot_general | solution.py:78
  163.2 11.3 %fusion.32 = f32[32,8,16,64]{3,0,2,1:T(8,128)S(1)} fusion(f32[8,16,64,128]{3,2,1,0:T(8,128)S(1)} %get-tuple-element.26, f32[32,128]{1,0:T(8,128)S(1)} %maximum_multiply_fusion), kind=kOutput, calls=%fused_computation.102 | convolution fusion | flops 402653184 | bytes 5259264 | tf_op jit(solution)/shard_map/ixyz,cz->cixy/dot_general | solution.py:56
  179.7 29.9 %all_to_all.69 = f32[8,1,32768]{2,1,0:T(1,128)} all-to-all(f32[8,1,32768]{2,1,0:T(1,128)S(1)} %reshape.43), channel_id=1, replica_groups=mesh['groups'=1,'gx'=8,'gy'=2,'segment'=2] {'gx'}, dimensions={0} | all-to-all | bytes 2097152 | tf_op jit(solution)/shard_map/all_to_all | solution.py:59
  222.5 7.1 %reduce-scatter.6.cloned.1.call-done = f32[16,4,8,32]{3,0,2,1:T(8,128)} async-done(((f32[32,4,8,32]{3,0,2,1:T(8,128)}), f32[16,4,8,32]{3,0,2,1:T(8,128)}) %reduce-scatter.6.cloned.1.call-update) | async-done | bytes 65552 | tf_op jit(solution)/shard_map/reduce_scatter | solution.py:63
  236.7 5.0 slice_bitcast_fusion.8
  271.6 5.8 %all-to-all-start.3 = ((f32[8,1,32768]{2,1,0:T(1,128)}), f32[8,1,32768]{2,1,0:T(1,128)}, u32[]{:S(2)}, u32[]{:S(2)}) async-start(f32[8,1,32768]{2,1,0:T(1,128)} %reshape.45), calls=%async_computation.5 | async-start | bytes 2097152 | tf_op jit(solution)/shard_map/all_to_all | solution.py:81
  277.6 7.2 %multiply_reduce_fusion.1 = f32[8,16,64,128]{3,2,1,0:T(8,128)} fusion(f32[8,16,64,128]{3,2,1,0:T(8,128)} %copy-done.1, f32[8,8]{1,0:T(8,128)S(1)} %copy.64), kind=kLoop, calls=%fused_computation.1 | loop fusion | flops 15728640 | bytes 8388864 | tf_op jit(solution)/shard_map/reduce_sum | solution.py:37
  284.8 18.9 %all-to-all-done.3 = f32[8,1,32768]{2,1,0:T(1,128)} async-done(((f32[8,1,32768]{2,1,0:T(1,128)}), f32[8,1,32768]{2,1,0:T(1,128)}, u32[]{:S(2)}, u32[]{:S(2)}) %all-to-all-start.3) | async-done | bytes 1048608 | tf_op jit(solution)/shard_map/all_to_all | solution.py:81
  313.3 7.1 %add_convert_fusion.1 = bf16[8,16,64,128]{3,2,1,0:T(8,128)(2,1)S(1)} fusion(f32[8,16,64,128]{3,2,1,0:T(8,128)S(1)} %copy-done.4, f32[32,8,16,64]{3,0,2,1:T(8,128)S(1)} %bitcast.179, f32[32,128]{1,0:T(8,128)S(1)} %maximum_multiply_fusion), kind=kOutput, calls=%fused_computation.10 | convolution fusion | flops 404750336 | bytes 7356416 | tf_op jit(solution)/shard_map/cixy,cz->ixyz/dot_general | solution.py:78
  321.9 47.1 %collective-permute-done = bf16[8,16,64,128]{3,2,1,0:T(8,128)(2,1)S(1)} collective-permute-done((bf16[8,16,64,128]{3,2,1,0:T(8,128)(2,1)S(1)}, bf16[8,16,64,128]{3,2,1,0:T(8,128)(2,1)S(1)}, u32[]{:S(2)}, u32[]{:S(2)}) %collective-permute-start) | collective-permute-done | bytes 2097184 | tf_op jit(solution)/shard_map/ppermute | solution.py:14
  370.1 11.3 %fusion.27 = f32[32,8,16,64]{3,0,2,1:T(8,128)S(1)} fusion(f32[8,16,64,128]{3,2,1,0:T(8,128)S(1)} %convert_multiply_fusion, f32[32,128]{1,0:T(8,128)S(1)} %maximum_multiply_fusion), kind=kOutput, calls=%fused_computation.97 | convolution fusion | flops 402653184 | bytes 5259264 | tf_op jit(solution)/shard_map/ixyz,cz->cixy/dot_general | solution.py:56
  386.6 29.9 %all_to_all.70 = f32[8,1,32768]{2,1,0:T(1,128)} all-to-all(f32[8,1,32768]{2,1,0:T(1,128)S(1)} %reshape.47), channel_id=1, replica_groups=mesh['groups'=1,'gx'=8,'gy'=2,'segment'=2] {'gx'}, dimensions={0} | all-to-all | bytes 2097152 | tf_op jit(solution)/shard_map/all_to_all | solution.py:59
  429.4 6.1 %reduce-scatter.8.cloned.1.call-done = f32[16,4,8,32]{3,0,2,1:T(8,128)} async-done(((f32[32,4,8,32]{3,0,2,1:T(8,128)}), f32[16,4,8,32]{3,0,2,1:T(8,128)}) %reduce-scatter.8.cloned.1.call-update) | async-done | bytes 65552 | tf_op jit(solution)/shard_map/reduce_scatter | solution.py:63
  468.0 6.0 %all-to-all-start.5 = ((f32[8,1,32768]{2,1,0:T(1,128)}), f32[8,1,32768]{2,1,0:T(1,128)S(1)}, u32[]{:S(2)}, u32[]{:S(2)}) async-start(f32[8,1,32768]{2,1,0:T(1,128)} %reshape.49), calls=%async_computation.8 | async-start | bytes 2097152 | tf_op jit(solution)/shard_map/all_to_all | solution.py:81
  474.0 7.2 %multiply_reduce_fusion = f32[8,16,64,128]{3,2,1,0:T(8,128)} fusion(f32[8,16,64,128]{3,2,1,0:T(8,128)} %copy-done, f32[8,8]{1,0:T(8,128)S(1)} %copy.64), kind=kLoop, calls=%fused_computation | loop fusion | flops 15728640 | bytes 8388864 | tf_op jit(solution)/shard_map/reduce_sum | solution.py:37
  483.0 17.2 %all-to-all-done.5 = f32[8,1,32768]{2,1,0:T(1,128)S(1)} async-done(((f32[8,1,32768]{2,1,0:T(1,128)}), f32[8,1,32768]{2,1,0:T(1,128)S(1)}, u32[]{:S(2)}, u32[]{:S(2)}) %all-to-all-start.5) | async-done | bytes 1048608 | tf_op jit(solution)/shard_map/all_to_all | solution.py:81
  506.4 8.0 %select_bitcast_fusion = bf16[1,8,16,64,128]{4,3,2,1,0:T(8,128)(2,1)} fusion(bf16[8,16,64,128]{3,2,1,0:T(8,128)(2,1)} %copy-done.7, pred[]{:T(512)S(6)} %eq.24, pred[]{:T(512)S(6)} %eq.22, f32[8,16,64,128]{3,2,1,0:T(8,128)S(1)} %copy-done.3, f32[32,8,16,64]{3,0,2,1:T(8,128)S(1)} %bitcast.178, f32[32,128]{1,0:T(8,128)S(1)} %maximum_multiply_fusion), kind=kOutput, calls=%fused_computation.22 | convolution fusion | flops 406847488 | bytes 9453570 | tf_op jit(solution)/shard_map/cixy,cz->ixyz/dot_general | solution.py:78
  (166 shorter events, 194.2 us)
Async XLA Ops:
  18.1 33.0 %all-to-all-start = ((f32[8,1,32768]{2,1,0:T(1,128)}), f32[8,1,32768]{2,1,0:T(1,128)S(1)}, u32[]{:S(2)}, u32[]{:S(2)}) async-start(f32[8,1,32768]{2,1,0:T(1,128)} %reshape.39), calls=%async_computation | async-start | bytes 2097152 | tf_op jit(solution)/shard_map/all_to_all | solution.py:59
  25.4 42.3 %reduce-scatter.4.cloned.1.call-start = ((), (), s32[]{:S(2)}) async-start(), calls=%async_computation.9 | async-start | bytes 786432 | tf_op jit(solution)/shard_map/reduce_scatter | solution.py:63
  56.0 12.7 %copy-start.2 = (f32[1,16,4,8,8,32]{5,4,3,2,1,0:T(8,128)S(1)}, f32[1,16,4,8,8,32]{5,4,3,2,1,0:T(8,128)}, u32[]{:S(2)}) copy-start(f32[1,16,4,8,8,32]{5,4,3,2,1,0:T(8,128)} %param.7) | copy-start | bytes 1572868
  96.5 6.8 %copy-start.18 = (f32[1,4,8,16,64]{4,3,2,1,0:T(8,128)S(1)}, f32[1,4,8,16,64]{4,3,2,1,0:T(8,128)}, u32[]{:S(2)}) copy-start(f32[1,4,8,16,64]{4,3,2,1,0:T(8,128)} %copy.73) | copy-start | bytes 393220
  96.5 7.5 %copy-start.15 = (f32[1,4,8,16,64]{4,3,2,1,0:T(8,128)S(1)}, f32[1,4,8,16,64]{4,3,2,1,0:T(8,128)}, u32[]{:S(2)}) copy-start(f32[1,4,8,16,64]{4,3,2,1,0:T(8,128)} %copy.74) | copy-start | bytes 393220
  96.5 8.2 %copy-start.12 = (f32[1,4,8,16,64]{4,3,2,1,0:T(8,128)S(1)}, f32[1,4,8,16,64]{4,3,2,1,0:T(8,128)}, u32[]{:S(2)}) copy-start(f32[1,4,8,16,64]{4,3,2,1,0:T(8,128)} %copy.75) | copy-start | bytes 393220
  96.5 9.0 %copy-start.9 = (f32[1,4,8,16,64]{4,3,2,1,0:T(8,128)S(1)}, f32[1,4,8,16,64]{4,3,2,1,0:T(8,128)}, u32[]{:S(2)}) copy-start(f32[1,4,8,16,64]{4,3,2,1,0:T(8,128)} %copy.76) | copy-start | bytes 393220
  109.6 32.1 %all-to-all-start.1 = ((f32[8,1,32768]{2,1,0:T(1,128)}), f32[8,1,32768]{2,1,0:T(1,128)}, u32[]{:S(2)}, u32[]{:S(2)}) async-start(f32[8,1,32768]{2,1,0:T(1,128)} %reshape.41), calls=%async_computation.2 | async-start | bytes 2097152 | tf_op jit(solution)/shard_map/all_to_all | solution.py:81
  115.3 114.4 %reduce-scatter.6.cloned.1.call-start = ((), (), s32[]{:S(2)}) async-start(), calls=%async_computation.10 | async-start | bytes 786432 | tf_op jit(solution)/shard_map/reduce_scatter | solution.py:63
  163.2 11.4 %copy-start.1 = (f32[8,16,64,128]{3,2,1,0:T(8,128)}, f32[8,16,64,128]{3,2,1,0:T(8,128)S(1)}, u32[]{:S(2)}) copy-start(f32[8,16,64,128]{3,2,1,0:T(8,128)S(1)} %get-tuple-element.26) | copy-start | bytes 12582916
  258.5 6.8 %copy-start.19 = (f32[1,4,8,16,64]{4,3,2,1,0:T(8,128)S(1)}, f32[1,4,8,16,64]{4,3,2,1,0:T(8,128)}, u32[]{:S(2)}) copy-start(f32[1,4,8,16,64]{4,3,2,1,0:T(8,128)} %copy.86) | copy-start | bytes 393220
  258.5 7.5 %copy-start.16 = (f32[1,4,8,16,64]{4,3,2,1,0:T(8,128)S(1)}, f32[1,4,8,16,64]{4,3,2,1,0:T(8,128)}, u32[]{:S(2)}) copy-start(f32[1,4,8,16,64]{4,3,2,1,0:T(8,128)} %copy.87) | copy-start | bytes 393220
  258.5 8.2 %copy-start.13 = (f32[1,4,8,16,64]{4,3,2,1,0:T(8,128)S(1)}, f32[1,4,8,16,64]{4,3,2,1,0:T(8,128)}, u32[]{:S(2)}) copy-start(f32[1,4,8,16,64]{4,3,2,1,0:T(8,128)} %copy.88) | copy-start | bytes 393220
  258.5 9.0 %copy-start.10 = (f32[1,4,8,16,64]{4,3,2,1,0:T(8,128)S(1)}, f32[1,4,8,16,64]{4,3,2,1,0:T(8,128)}, u32[]{:S(2)}) copy-start(f32[1,4,8,16,64]{4,3,2,1,0:T(8,128)} %copy.89) | copy-start | bytes 393220
  271.6 32.1 %all-to-all-start.3 = ((f32[8,1,32768]{2,1,0:T(1,128)}), f32[8,1,32768]{2,1,0:T(1,128)}, u32[]{:S(2)}, u32[]{:S(2)}) async-start(f32[8,1,32768]{2,1,0:T(1,128)} %reshape.45), calls=%async_computation.5 | async-start | bytes 2097152 | tf_op jit(solution)/shard_map/all_to_all | solution.py:81
  277.3 158.3 %reduce-scatter.8.cloned.1.call-start = ((), (), s32[]{:S(2)}) async-start(), calls=%async_computation.11 | async-start | bytes 786432 | tf_op jit(solution)/shard_map/reduce_scatter | solution.py:63
  313.3 55.7 %copy-start.5 = (f32[8,16,64,128]{3,2,1,0:T(8,128)S(1)}, f32[8,16,64,128]{3,2,1,0:T(8,128)}, u32[]{:S(2)}) copy-start(f32[8,16,64,128]{3,2,1,0:T(8,128)} %get-tuple-element.27) | copy-start | bytes 12582916
  320.4 48.6 %copy-start.7 = (bf16[8,16,64,128]{3,2,1,0:T(8,128)(2,1)}, bf16[8,16,64,128]{3,2,1,0:T(8,128)(2,1)S(1)}, u32[]{:S(2)}) copy-start(bf16[8,16,64,128]{3,2,1,0:T(8,128)(2,1)S(1)} %add_convert_fusion.1) | copy-start | bytes 6291460
  320.4 48.6 %collective-permute-start = (bf16[8,16,64,128]{3,2,1,0:T(8,128)(2,1)S(1)}, bf16[8,16,64,128]{3,2,1,0:T(8,128)(2,1)S(1)}, u32[]{:S(2)}, u32[]{:S(2)}) collective-permute-start(bf16[8,16,64,128]{3,2,1,0:T(8,128)(2,1)S(1)} %add_convert_fusion.1), channel_id=1, source_target_pairs={{1,0},{3,2},{5,4},{7,6},{9,8},{11,10},{13,12},{15,14},{17,16},{19,... | collective-permute-start | bytes 6291464 | tf_op jit(solution)/shard_map/ppermute | solution.py:14
  370.1 11.4 %copy-start = (f32[8,16,64,128]{3,2,1,0:T(8,128)}, f32[8,16,64,128]{3,2,1,0:T(8,128)S(1)}, u32[]{:S(2)}) copy-start(f32[8,16,64,128]{3,2,1,0:T(8,128)S(1)} %convert_multiply_fusion) | copy-start | bytes 12582916
  451.8 6.9 %copy-start.8 = (f32[1,4,8,16,64]{3,4,2,1,0:T(8,128)S(1)}, f32[1,4,8,16,64]{3,4,2,1,0:T(8,128)}, u32[]{:S(2)}) copy-start(f32[1,4,8,16,64]{3,4,2,1,0:T(8,128)} %get-tuple-element.7) | copy-start | bytes 393220
  468.0 32.2 %all-to-all-start.5 = ((f32[8,1,32768]{2,1,0:T(1,128)}), f32[8,1,32768]{2,1,0:T(1,128)S(1)}, u32[]{:S(2)}, u32[]{:S(2)}) async-start(f32[8,1,32768]{2,1,0:T(1,128)} %reshape.49), calls=%async_computation.8 | async-start | bytes 2097152 | tf_op jit(solution)/shard_map/all_to_all | solution.py:81
  474.0 7.2 %copy-start.21 = (f32[16,4,8,32]{3,0,2,1:T(8,128)S(1)}, f32[16,4,8,32]{3,0,2,1:T(8,128)}, u32[]{:S(2)}) copy-start(f32[16,4,8,32]{3,0,2,1:T(8,128)} %reduce-scatter.6.cloned.1.call-done) | copy-start | bytes 196612
  474.0 7.2 %copy-start.22 = (f32[16,4,8,32]{3,0,2,1:T(8,128)S(1)}, f32[16,4,8,32]{3,0,2,1:T(8,128)}, u32[]{:S(2)}) copy-start(f32[16,4,8,32]{3,0,2,1:T(8,128)} %reduce-scatter.8.cloned.1.call-done) | copy-start | bytes 196612
  (9 other events, 34.8 us)
Sparse Core Ops, SparseCore 0:
  60.7 6.9 reduce-scatter.3
  222.6 6.9 reduce-scatter.5
  429.5 5.9 reduce-scatter.7
